TPU v7x, 32 devices: a whole 2x2x4 slice. The times are simulated.
32 devices in a mesh: section: 4 (over x, core), win: 8 (over z, y).
Axes of the slice: x: 2, y: 2, z: 4, core: 2. Of those that a mesh axis runs over, the one named last changes fastest.
Arguments:
- latent: bfloat16 [24, 64, 256], P(None, 'win'), may hold values from -6 to 6
- anchors: int32 [16, 2], P('win'), may hold values from 0 to 56, as said below
- in_proj: bfloat16 [256, 1280], replicated, may hold values from -0.375 to 0.375
- pos_embed: bfloat16 [256, 1280], replicated, may hold values from -6 to 6
- section_w1: bfloat16 [4, 1280, 2560], P('section'), may hold values from -0.15625 to 0.15625
- section_w2: bfloat16 [4, 2560, 1280], P('section'), may hold values from -0.125 to 0.125
- section_gain: float32 [4, 1280], P('section'), may hold values from 0.5 to 1.5
- skip_w: bfloat16 [2560, 1280], replicated, may hold values from -0.125 to 0.125
- out_proj: bfloat16 [1280, 256], replicated, may hold values from -0.15625 to 0.15625
Outputs:
- noise_avg: bfloat16 [24, 64, 256], P('section', 'win')
Inputs may be any that keep to these rules, and one draw needn't show every extreme that they name: Column 0 holds the row anchor, column 1 the column anchor; the windows are listed in an order drawn at random. Every column anchor that is a multiple of 8 below 64 appears in exactly 2 windows. Let g be a column anchor divided by 8. For even g, the row anchors of those windows are 0 and 8. For odd g, each row anchor lies anywhere from 0 to 8. Every token is covered by at least one window.
All inputs are finite; a program needn't handle non-finite values.
Results may differ from a plain program's by a relative error of at most 0.014.
Values may be sent and summed in bfloat16 or wider, within the bound.
A program may use at most 128 MiB of HBM per device.

v0:
```python
import jax
import jax.numpy as jnp
from jax import lax
from jax.sharding import PartitionSpec as P

TILE = 16
MB = 1


def shortened(shard):
    return jax.tree.map(lambda a: a.astype(jnp.bfloat16) if a.dtype == jnp.float32 else a, shard)


def shifted(value, axis, steps):
    count = lax.axis_size(axis)
    leading, last = (max(0, -steps), min(count, count - steps))
    return lax.ppermute(value, axis, [(source, source + steps) for source in range(leading, last)])


def rms_block(values, gain, w_first, w_second):
    factor = lax.rsqrt(jnp.mean(values * values, axis=-1, keepdims=True) + 1e-06)
    normed = (values * factor * gain).astype(jnp.bfloat16)
    hidden = jax.nn.gelu(
        jnp.dot(normed, w_first, preferred_element_type=jnp.float32), approximate=True
    ).astype(jnp.bfloat16)
    return values + jnp.dot(hidden, w_second, preferred_element_type=jnp.float32)


def per_device(
    latent, anchors, in_proj, pos_embed, section_w1, section_w2, section_gain, skip_w, out_proj
):
    section_id = lax.axis_index("section")
    sections = lax.axis_size("section")
    slabs = lax.axis_size("win")
    w_first = section_w1[0]
    w_second = section_w2[0]
    gain = section_gain[0]
    panorama = lax.all_gather(latent, "win", axis=1, tiled=True)
    height, width, feat_dim = panorama.shape
    slab_width = latent.shape[1]
    model_dim = in_proj.shape[1]
    win_count = anchors.shape[0]
    micro_count = win_count // MB
    row_count = MB * TILE * TILE
    offsets = jnp.arange(TILE, dtype=jnp.int32)
    position_term = jnp.tile(pos_embed.astype(jnp.float32), (MB, 1))
    zeros_noise = jnp.zeros((row_count, feat_dim), jnp.bfloat16)
    zeros_act = jnp.zeros((row_count, model_dim), jnp.bfloat16)

    def window_tokens(picked):
        row_index = picked[:, 0:1] + offsets[None, :]
        col_index = (picked[:, 1:2] + offsets[None, :]) % width
        tiles = panorama[row_index[:, :, None], col_index[:, None, :]]
        return tiles.reshape(row_count, feat_dim)

    def first_section(received, skipped, index):
        picked = lax.dynamic_slice_in_dim(anchors, index * MB, MB, 0)
        embedded = (
            jnp.dot(window_tokens(picked), in_proj, preferred_element_type=jnp.float32)
            + position_term
        )
        return (rms_block(embedded, gain, w_first, w_second).astype(jnp.bfloat16), zeros_noise)

    def middle_section(received, skipped, index):
        return (
            rms_block(received.astype(jnp.float32), gain, w_first, w_second).astype(jnp.bfloat16),
            zeros_noise,
        )

    def last_section(received, skipped, index):
        joined = jnp.concatenate([received, skipped], axis=1)
        merged = jnp.dot(joined, skip_w, preferred_element_type=jnp.float32)
        deep = rms_block(merged, gain, w_first, w_second).astype(jnp.bfloat16)
        return (
            deep,
            jnp.dot(deep, out_proj, preferred_element_type=jnp.float32).astype(jnp.bfloat16),
        )

    branches = [first_section] + [middle_section] * (sections - 2) + [last_section]

    def run_section(tick, received, skipped, noises):
        index = jnp.clip(tick - section_id, 0, micro_count - 1)
        produced, noise = lax.switch(section_id, branches, received, skipped, index)
        noises = lax.dynamic_update_index_in_dim(noises, noise, index, 0)
        return (produced, noises)

    ticks = micro_count + sections - 1
    noise_init = jnp.zeros((micro_count, row_count, feat_dim), jnp.bfloat16)

    def advance_direct(tick, carry):
        received, queue, noises = carry
        produced, noises = run_section(tick, received, queue[0], noises)
        received = jax.tree.map(
            lambda part, own: part.astype(own.dtype),
            shifted(shortened(produced), "section", 1),
            produced,
        )
        arrived = jax.tree.map(
            lambda part, own: part.astype(own.dtype),
            shifted(shortened(produced), "section", sections - 1),
            produced,
        )
        queue = jnp.concatenate([queue[1:], arrived[None]], axis=0)
        return (received, queue, noises)

    queue_init = jnp.zeros((sections - 1, row_count, model_dim), jnp.bfloat16)
    noises = lax.fori_loop(0, ticks, advance_direct, (zeros_act, queue_init, noise_init))[2]
    live = (section_id == sections - 1).astype(jnp.float32)
    band = height // sections
    placed = noises.reshape(win_count, TILE, TILE, feat_dim).astype(jnp.float32)
    row_index = anchors[:, 0:1] + offsets[None, :]
    col_index = (anchors[:, 1:2] + offsets[None, :]) % width
    band_high = (row_index // band)[:, :, None]
    band_low = (row_index % band)[:, :, None]
    slab_high = (col_index // slab_width)[:, None, :]
    slab_low = (col_index % slab_width)[:, None, :]
    sums = jnp.zeros((sections, slabs, band, slab_width, feat_dim), jnp.float32)
    sums = sums.at[band_high, slab_high, band_low, slab_low].add(placed)
    counts = jnp.zeros((sections, slabs, band, slab_width), jnp.float32)
    counts = counts.at[band_high, slab_high, band_low, slab_low].add(live)
    totals, covered = (
        lax.psum_scatter(
            sums.reshape(sections * slabs, band, slab_width, feat_dim),
            ("section", "win"),
            scatter_dimension=0,
            tiled=True,
        ),
        lax.psum_scatter(
            counts.reshape(sections * slabs, band, slab_width),
            ("section", "win"),
            scatter_dimension=0,
            tiled=True,
        ),
    )
    return (totals[0] / covered[0][..., None]).astype(jnp.bfloat16)


def solution(mesh):
    placed = (
        P(None, "win", None),
        P("win", None),
        P(),
        P(),
        P("section", None, None),
        P("section", None, None),
        P("section", None),
        P(),
        P(),
    )
    return jax.shard_map(
        per_device, mesh=mesh, in_specs=placed, out_specs=P("section", "win", None), check_vma=False
    )
```

profile of v0, /device:TPU:0, one launch (start us, length us, event | category | flops | bytes accessed | tf_op | source)
XLA Modules:
  0.0 355.0 jit_solution(2862663881316935435)
XLA Ops:
  6.5 1.0 slice_reduce_fusion.1
  8.5 1.2 convert_element_type.62
  9.7 36.2 %all_gather.3 = bf16[24,64,256]{2,1,0:T(8,128)(2,1)} all-gather(bf16[24,8,256]{2,1,0:T(8,128)(2,1)} %param.15), channel_id=1, replica_groups=mesh['section'=4,'win'=8] {'win'}, dimensions={1}, use_global_device_ids=true | all-gather | bytes 884736 | tf_op jit(solution)/shard_map/all_gather | solution.py:38
  45.9 1.4 broadcast_in_dim.110
  47.4 0.7 broadcast_in_dim.111
  48.1 158.9 %while.20 = (s32[]{:T(128)}, bf16[256,1280]{1,0:T(8,128)(2,1)S(1)}, bf16[3,256,1280]{2,1,0:T(8,128)(2,1)}, bf16[2,256,256]{2,1,0:T(8,128)(2,1)}, s32[]{:T(128)},...) while((s32[]{:T(128)}, bf16[256,1280]{1,0:T(8,128)(2,1)S(1)}, ...), condition=%wide.region_9.10_spmd.clone.clone, body=%wide.region_0.9_spmd.clone.clone.sunk | while | flops 5212798976 | bytes 39079948 | solution.py:107
  48.1 15.7 %conditional.14 = (bf16[1,256,256]{2,1,0:T(8,128)(2,1)S(1)}, bf16[256,1280]{1,0:T(8,128)(2,1)}) conditional(s32[]{:T(128)} %get-tuple-element.683, (s32[]{:T(128)}, s32[2,2]{1,0:T(2,128)S(1)}, s32[16]{0:T(128)S(1)}, s32[16]{0:T(128)S(1)}, bf16[24,64,256]{2,1,0:T(8,128)(2,1)}, /*index=5*/bf16[256,1280]{1,0:T(8,128)(2,1)}, ...), branch_computations={%region_1.2_spmd, %region_3.4_spmd, %region_5.6_spmd, %region_7.8_... | conditional | flops 5211815936 | bytes 27020308
  48.7 1.3 compare_select_fusion
  50.1 2.7 gather_fusion
  52.9 1.5 multiply_reduce_fusion.1
  54.4 9.3 %convolution_add_fusion.4 = bf16[256,1280]{1,0:T(8,128)(2,1)} fusion(f32[256,1280]{1,0:T(8,128)S(1)} %get-tuple-element.517, bf16[2560,1280]{1,0:T(8,128)(2,1)} %get-tuple-element.366, bf16[1280,2560]{1,0:T(8,128)(2,1)} %get-tuple-element.365, f32[1280]{0:T(1024)S(1)} %reduce.3, f32[256]{0:T(256)S(1)} %add_rsqrt_fusion.3), kind=kOutput, calls=%fused_computation.93 | convolution fusion | flops 3362979840 | bytes 15079424 | tf_op jit(solution)/shard_map/while/body/eval_jaxpr/cond/branch_0_fun/dot_general | solution.py:26
  63.8 2.2 collective-permute-start.1
  65.9 1.3 collective-permute-start
  67.3 1.4 slice.64
  68.7 0.7 constant_dynamic-update-slice_fusion.2
  69.3 8.2 %collective-permute-done.1 = bf16[256,1280]{1,0:T(8,128)(2,1)} collective-permute-done((bf16[256,1280]{1,0:T(8,128)(2,1)}, bf16[256,1280]{1,0:T(8,128)(2,1)}, u32[]{:S(2)}, u32[]{:S(2)}) %collective-permute-start.1) | collective-permute-done | bytes 655392 | tf_op jit(solution)/shard_map/while/body/eval_jaxpr/ppermute | solution.py:17
  77.5 2.5 pad_maximum_fusion.2
  80.1 15.7 %conditional.14 = (bf16[1,256,256]{2,1,0:T(8,128)(2,1)S(1)}, bf16[256,1280]{1,0:T(8,128)(2,1)}) conditional(s32[]{:T(128)} %get-tuple-element.683, (s32[]{:T(128)}, s32[2,2]{1,0:T(2,128)S(1)}, s32[16]{0:T(128)S(1)}, s32[16]{0:T(128)S(1)}, bf16[24,64,256]{2,1,0:T(8,128)(2,1)}, /*index=5*/bf16[256,1280]{1,0:T(8,128)(2,1)}, ...), branch_computations={%region_1.2_spmd, %region_3.4_spmd, %region_5.6_spmd, %region_7.8_... | conditional | flops 5211815936 | bytes 27020308
  80.7 1.3 compare_select_fusion
  82.1 2.7 gather_fusion
  84.8 1.5 multiply_reduce_fusion.1
  86.4 9.3 %convolution_add_fusion.4 = bf16[256,1280]{1,0:T(8,128)(2,1)} fusion(f32[256,1280]{1,0:T(8,128)S(1)} %get-tuple-element.517, bf16[2560,1280]{1,0:T(8,128)(2,1)} %get-tuple-element.366, bf16[1280,2560]{1,0:T(8,128)(2,1)} %get-tuple-element.365, f32[1280]{0:T(1024)S(1)} %reduce.3, f32[256]{0:T(256)S(1)} %add_rsqrt_fusion.3), kind=kOutput, calls=%fused_computation.93 | convolution fusion | flops 3362979840 | bytes 15079424 | tf_op jit(solution)/shard_map/while/body/eval_jaxpr/cond/branch_0_fun/dot_general | solution.py:26
  95.8 5.9 %collective-permute-start.1 = (bf16[256,1280]{1,0:T(8,128)(2,1)}, bf16[256,1280]{1,0:T(8,128)(2,1)}, u32[]{:S(2)}, u32[]{:S(2)}) collective-permute-start(bf16[256,1280]{1,0:T(8,128)(2,1)} %get-tuple-element.625), channel_id=1, source_target_pairs={{0,24},{1,25},{2,26},{3,27},{4,28},{5,29},{6,30},{7,31}} | collective-permute-start | bytes 1966088 | tf_op jit(solution)/shard_map/while/body/eval_jaxpr/ppermute | solution.py:17
  101.7 1.3 collective-permute-start
  103.0 1.4 slice.64
  105.1 4.2 %collective-permute-done.1 = bf16[256,1280]{1,0:T(8,128)(2,1)} collective-permute-done((bf16[256,1280]{1,0:T(8,128)(2,1)}, bf16[256,1280]{1,0:T(8,128)(2,1)}, u32[]{:S(2)}, u32[]{:S(2)}) %collective-permute-start.1) | collective-permute-done | bytes 655392 | tf_op jit(solution)/shard_map/while/body/eval_jaxpr/ppermute | solution.py:17
  109.2 2.5 pad_maximum_fusion.2
  111.8 15.7 %conditional.14 = (bf16[1,256,256]{2,1,0:T(8,128)(2,1)S(1)}, bf16[256,1280]{1,0:T(8,128)(2,1)}) conditional(s32[]{:T(128)} %get-tuple-element.683, (s32[]{:T(128)}, s32[2,2]{1,0:T(2,128)S(1)}, s32[16]{0:T(128)S(1)}, s32[16]{0:T(128)S(1)}, bf16[24,64,256]{2,1,0:T(8,128)(2,1)}, /*index=5*/bf16[256,1280]{1,0:T(8,128)(2,1)}, ...), branch_computations={%region_1.2_spmd, %region_3.4_spmd, %region_5.6_spmd, %region_7.8_... | conditional | flops 5211815936 | bytes 27020308
  112.4 1.3 compare_select_fusion
  113.8 2.7 gather_fusion
  116.6 1.5 multiply_reduce_fusion.1
  118.1 9.3 %convolution_add_fusion.4 = bf16[256,1280]{1,0:T(8,128)(2,1)} fusion(f32[256,1280]{1,0:T(8,128)S(1)} %get-tuple-element.517, bf16[2560,1280]{1,0:T(8,128)(2,1)} %get-tuple-element.366, bf16[1280,2560]{1,0:T(8,128)(2,1)} %get-tuple-element.365, f32[1280]{0:T(1024)S(1)} %reduce.3, f32[256]{0:T(256)S(1)} %add_rsqrt_fusion.3), kind=kOutput, calls=%fused_computation.93 | convolution fusion | flops 3362979840 | bytes 15079424 | tf_op jit(solution)/shard_map/while/body/eval_jaxpr/cond/branch_0_fun/dot_general | solution.py:26
  127.5 5.9 %collective-permute-start.1 = (bf16[256,1280]{1,0:T(8,128)(2,1)}, bf16[256,1280]{1,0:T(8,128)(2,1)}, u32[]{:S(2)}, u32[]{:S(2)}) collective-permute-start(bf16[256,1280]{1,0:T(8,128)(2,1)} %get-tuple-element.625), channel_id=1, source_target_pairs={{0,24},{1,25},{2,26},{3,27},{4,28},{5,29},{6,30},{7,31}} | collective-permute-start | bytes 1966088 | tf_op jit(solution)/shard_map/while/body/eval_jaxpr/ppermute | solution.py:17
  133.4 1.3 collective-permute-start
  134.7 1.4 slice.64
  136.8 4.2 %collective-permute-done.1 = bf16[256,1280]{1,0:T(8,128)(2,1)} collective-permute-done((bf16[256,1280]{1,0:T(8,128)(2,1)}, bf16[256,1280]{1,0:T(8,128)(2,1)}, u32[]{:S(2)}, u32[]{:S(2)}) %collective-permute-start.1) | collective-permute-done | bytes 655392 | tf_op jit(solution)/shard_map/while/body/eval_jaxpr/ppermute | solution.py:17
  141.0 2.5 pad_maximum_fusion.2
  143.5 15.7 %conditional.14 = (bf16[1,256,256]{2,1,0:T(8,128)(2,1)S(1)}, bf16[256,1280]{1,0:T(8,128)(2,1)}) conditional(s32[]{:T(128)} %get-tuple-element.683, (s32[]{:T(128)}, s32[2,2]{1,0:T(2,128)S(1)}, s32[16]{0:T(128)S(1)}, s32[16]{0:T(128)S(1)}, bf16[24,64,256]{2,1,0:T(8,128)(2,1)}, /*index=5*/bf16[256,1280]{1,0:T(8,128)(2,1)}, ...), branch_computations={%region_1.2_spmd, %region_3.4_spmd, %region_5.6_spmd, %region_7.8_... | conditional | flops 5211815936 | bytes 27020308
  144.1 1.3 compare_select_fusion
  145.5 2.7 gather_fusion
  148.3 1.5 multiply_reduce_fusion.1
  149.8 9.3 %convolution_add_fusion.4 = bf16[256,1280]{1,0:T(8,128)(2,1)} fusion(f32[256,1280]{1,0:T(8,128)S(1)} %get-tuple-element.517, bf16[2560,1280]{1,0:T(8,128)(2,1)} %get-tuple-element.366, bf16[1280,2560]{1,0:T(8,128)(2,1)} %get-tuple-element.365, f32[1280]{0:T(1024)S(1)} %reduce.3, f32[256]{0:T(256)S(1)} %add_rsqrt_fusion.3), kind=kOutput, calls=%fused_computation.93 | convolution fusion | flops 3362979840 | bytes 15079424 | tf_op jit(solution)/shard_map/while/body/eval_jaxpr/cond/branch_0_fun/dot_general | solution.py:26
  159.2 5.9 %collective-permute-start.1 = (bf16[256,1280]{1,0:T(8,128)(2,1)}, bf16[256,1280]{1,0:T(8,128)(2,1)}, u32[]{:S(2)}, u32[]{:S(2)}) collective-permute-start(bf16[256,1280]{1,0:T(8,128)(2,1)} %get-tuple-element.625), channel_id=1, source_target_pairs={{0,24},{1,25},{2,26},{3,27},{4,28},{5,29},{6,30},{7,31}} | collective-permute-start | bytes 1966088 | tf_op jit(solution)/shard_map/while/body/eval_jaxpr/ppermute | solution.py:17
  165.1 1.3 collective-permute-start
  166.5 1.4 slice.64
  168.5 4.2 %collective-permute-done.1 = bf16[256,1280]{1,0:T(8,128)(2,1)} collective-permute-done((bf16[256,1280]{1,0:T(8,128)(2,1)}, bf16[256,1280]{1,0:T(8,128)(2,1)}, u32[]{:S(2)}, u32[]{:S(2)}) %collective-permute-start.1) | collective-permute-done | bytes 655392 | tf_op jit(solution)/shard_map/while/body/eval_jaxpr/ppermute | solution.py:17
  172.7 2.5 pad_maximum_fusion.2
  175.2 15.7 %conditional.14 = (bf16[1,256,256]{2,1,0:T(8,128)(2,1)S(1)}, bf16[256,1280]{1,0:T(8,128)(2,1)}) conditional(s32[]{:T(128)} %get-tuple-element.683, (s32[]{:T(128)}, s32[2,2]{1,0:T(2,128)S(1)}, s32[16]{0:T(128)S(1)}, s32[16]{0:T(128)S(1)}, bf16[24,64,256]{2,1,0:T(8,128)(2,1)}, /*index=5*/bf16[256,1280]{1,0:T(8,128)(2,1)}, ...), branch_computations={%region_1.2_spmd, %region_3.4_spmd, %region_5.6_spmd, %region_7.8_... | conditional | flops 5211815936 | bytes 27020308
  175.8 1.3 compare_select_fusion
  177.3 2.7 gather_fusion
  180.0 1.5 multiply_reduce_fusion.1
  181.6 9.3 %convolution_add_fusion.4 = bf16[256,1280]{1,0:T(8,128)(2,1)} fusion(f32[256,1280]{1,0:T(8,128)S(1)} %get-tuple-element.517, bf16[2560,1280]{1,0:T(8,128)(2,1)} %get-tuple-element.366, bf16[1280,2560]{1,0:T(8,128)(2,1)} %get-tuple-element.365, f32[1280]{0:T(1024)S(1)} %reduce.3, f32[256]{0:T(256)S(1)} %add_rsqrt_fusion.3), kind=kOutput, calls=%fused_computation.93 | convolution fusion | flops 3362979840 | bytes 15079424 | tf_op jit(solution)/shard_map/while/body/eval_jaxpr/cond/branch_0_fun/dot_general | solution.py:26
  190.9 5.9 %collective-permute-start.1 = (bf16[256,1280]{1,0:T(8,128)(2,1)}, bf16[256,1280]{1,0:T(8,128)(2,1)}, u32[]{:S(2)}, u32[]{:S(2)}) collective-permute-start(bf16[256,1280]{1,0:T(8,128)(2,1)} %get-tuple-element.625), channel_id=1, source_target_pairs={{0,24},{1,25},{2,26},{3,27},{4,28},{5,29},{6,30},{7,31}} | collective-permute-start | bytes 1966088 | tf_op jit(solution)/shard_map/while/body/eval_jaxpr/ppermute | solution.py:17
  196.9 1.3 collective-permute-start
  198.2 1.4 slice.64
  200.2 4.2 %collective-permute-done.1 = bf16[256,1280]{1,0:T(8,128)(2,1)} collective-permute-done((bf16[256,1280]{1,0:T(8,128)(2,1)}, bf16[256,1280]{1,0:T(8,128)(2,1)}, u32[]{:S(2)}, u32[]{:S(2)}) %collective-permute-start.1) | collective-permute-done | bytes 655392 | tf_op jit(solution)/shard_map/while/body/eval_jaxpr/ppermute | solution.py:17
  204.4 2.5 pad_maximum_fusion.2
  206.9 1.0 bitcast_convert_fusion
  208.1 38.8 %scatter_fusion = f32[4,8,6,8,256]{4,3,2,1,0:T(8,128)S(1)} fusion(f32[4,8,6,8,256]{4,3,2,1,0:T(8,128)S(1)} %broadcast_in_dim.68, s32[512]{0:T(512)S(1)} %copy-done, f32[512,256]{1,0:T(8,128)S(1)} %bitcast_convert_fusion), kind=kCustom, calls=%fused_computation.1 | custom fusion | flops 131072 | bytes 1581056 | tf_op jit(solution)/shard_map/scatter-add | solution.py:118
  246.9 1.1 copy-done.1
  248.1 35.2 %scatter_fusion.1 = f32[4,8,6,8]{3,1,2,0:T(8,128)S(1)} fusion(f32[4,8,6,8]{3,1,2,0:T(8,128)S(1)} %broadcast_in_dim.112, s32[512]{0:T(512)S(1)} %copy-done, f32[512]{0:T(512)S(1)} %broadcast.423), kind=kCustom, calls=%fused_computation.2 | custom fusion | flops 512 | bytes 14336 | tf_op jit(solution)/shard_map/scatter-add | solution.py:120
  283.4 39.8 %all-reduce = f32[32,6,8]{2,1,0:T(8,128)S(1)} all-reduce(f32[32,6,8]{2,1,0:T(8,128)S(1)} %bitcast.44), channel_id=3, replica_groups=mesh['section'=4,'win'=8] {'section','win'}, use_global_device_ids=true, to_apply=%region_13.14.clone | all-reduce | flops 1536 | bytes 12288
  323.2 23.5 %reduce-scatter.2.cloned.1.call-done = f32[1,6,8,256]{3,2,1,0:T(8,128)} async-done(((f32[32,6,8,256]{3,2,1,0:T(8,128)}), f32[1,6,8,256]{3,2,1,0:T(8,128)}) %reduce-scatter.2.cloned.1.call-update) | async-done | bytes 49168 | tf_op jit(solution)/shard_map/reduce_scatter | solution.py:122
  346.7 1.5 fusion.117
  (83 shorter events, 7.9 us)
Async XLA Ops:
  6.5 340.1 %reduce-scatter.2.cloned.1.call-start = ((), (), s32[]{:S(2)}) async-start(), calls=%async_computation.1 | async-start | bytes 1622016 | tf_op jit(solution)/shard_map/reduce_scatter | solution.py:122
  8.5 39.6 %copy-start.2 = (f32[1,1280]{1,0:T(1,128)S(1)}, f32[1,1280]{1,0:T(1,128)}, u32[]{:S(2)}) copy-start(f32[1,1280]{1,0:T(1,128)} %param.21) | copy-start | bytes 15364
  8.5 39.6 %copy-start.3 = (s32[2,2]{1,0:T(2,128)S(1)}, s32[2,2]{1,0:T(2,128)}, u32[]{:S(2)}) copy-start(s32[2,2]{1,0:T(2,128)} %param.16) | copy-start | bytes 52
  48.1 160.0 %copy-start = (s32[512]{0:T(512)S(1)}, s32[512]{0:T(512)}, u32[]{:S(2)}) copy-start(s32[512]{0:T(512)} %reshape.216) | copy-start | bytes 6148
  63.8 13.7 %collective-permute-start.1 = (bf16[256,1280]{1,0:T(8,128)(2,1)}, bf16[256,1280]{1,0:T(8,128)(2,1)}, u32[]{:S(2)}, u32[]{:S(2)}) collective-permute-start(bf16[256,1280]{1,0:T(8,128)(2,1)} %get-tuple-element.625), channel_id=1, source_target_pairs={{0,24},{1,25},{2,26},{3,27},{4,28},{5,29},{6,30},{7,31}} | collective-permute-start | bytes 1966088 | tf_op jit(solution)/shard_map/while/body/eval_jaxpr/ppermute | solution.py:17
  65.9 14.1 %collective-permute-start = (bf16[256,1280]{1,0:T(8,128)(2,1)}, bf16[256,1280]{1,0:T(8,128)(2,1)S(1)}, u32[]{:S(2)}, u32[]{:S(2)}) collective-permute-start(bf16[256,1280]{1,0:T(8,128)(2,1)} %get-tuple-element.625), channel_id=1, source_target_pairs={{0,8},{8,16},{16,24},{1,9},{9,17},{17,25},{2,10},{10,18},{18,26},{... | collective-permute-start | bytes 1966088 | tf_op jit(solution)/shard_map/while/body/eval_jaxpr/ppermute | solution.py:17
  95.8 13.5 %collective-permute-start.1 = (bf16[256,1280]{1,0:T(8,128)(2,1)}, bf16[256,1280]{1,0:T(8,128)(2,1)}, u32[]{:S(2)}, u32[]{:S(2)}) collective-permute-start(bf16[256,1280]{1,0:T(8,128)(2,1)} %get-tuple-element.625), channel_id=1, source_target_pairs={{0,24},{1,25},{2,26},{3,27},{4,28},{5,29},{6,30},{7,31}} | collective-permute-start | bytes 1966088 | tf_op jit(solution)/shard_map/while/body/eval_jaxpr/ppermute | solution.py:17
  101.7 10.1 %collective-permute-start = (bf16[256,1280]{1,0:T(8,128)(2,1)}, bf16[256,1280]{1,0:T(8,128)(2,1)S(1)}, u32[]{:S(2)}, u32[]{:S(2)}) collective-permute-start(bf16[256,1280]{1,0:T(8,128)(2,1)} %get-tuple-element.625), channel_id=1, source_target_pairs={{0,8},{8,16},{16,24},{1,9},{9,17},{17,25},{2,10},{10,18},{18,26},{... | collective-permute-start | bytes 1966088 | tf_op jit(solution)/shard_map/while/body/eval_jaxpr/ppermute | solution.py:17
  127.5 13.5 %collective-permute-start.1 = (bf16[256,1280]{1,0:T(8,128)(2,1)}, bf16[256,1280]{1,0:T(8,128)(2,1)}, u32[]{:S(2)}, u32[]{:S(2)}) collective-permute-start(bf16[256,1280]{1,0:T(8,128)(2,1)} %get-tuple-element.625), channel_id=1, source_target_pairs={{0,24},{1,25},{2,26},{3,27},{4,28},{5,29},{6,30},{7,31}} | collective-permute-start | bytes 1966088 | tf_op jit(solution)/shard_map/while/body/eval_jaxpr/ppermute | solution.py:17
  133.4 10.1 %collective-permute-start = (bf16[256,1280]{1,0:T(8,128)(2,1)}, bf16[256,1280]{1,0:T(8,128)(2,1)S(1)}, u32[]{:S(2)}, u32[]{:S(2)}) collective-permute-start(bf16[256,1280]{1,0:T(8,128)(2,1)} %get-tuple-element.625), channel_id=1, source_target_pairs={{0,8},{8,16},{16,24},{1,9},{9,17},{17,25},{2,10},{10,18},{18,26},{... | collective-permute-start | bytes 1966088 | tf_op jit(solution)/shard_map/while/body/eval_jaxpr/ppermute | solution.py:17
  159.2 13.5 %collective-permute-start.1 = (bf16[256,1280]{1,0:T(8,128)(2,1)}, bf16[256,1280]{1,0:T(8,128)(2,1)}, u32[]{:S(2)}, u32[]{:S(2)}) collective-permute-start(bf16[256,1280]{1,0:T(8,128)(2,1)} %get-tuple-element.625), channel_id=1, source_target_pairs={{0,24},{1,25},{2,26},{3,27},{4,28},{5,29},{6,30},{7,31}} | collective-permute-start | bytes 1966088 | tf_op jit(solution)/shard_map/while/body/eval_jaxpr/ppermute | solution.py:17
  165.1 10.1 %collective-permute-start = (bf16[256,1280]{1,0:T(8,128)(2,1)}, bf16[256,1280]{1,0:T(8,128)(2,1)S(1)}, u32[]{:S(2)}, u32[]{:S(2)}) collective-permute-start(bf16[256,1280]{1,0:T(8,128)(2,1)} %get-tuple-element.625), channel_id=1, source_target_pairs={{0,8},{8,16},{16,24},{1,9},{9,17},{17,25},{2,10},{10,18},{18,26},{... | collective-permute-start | bytes 1966088 | tf_op jit(solution)/shard_map/while/body/eval_jaxpr/ppermute | solution.py:17
  190.9 13.5 %collective-permute-start.1 = (bf16[256,1280]{1,0:T(8,128)(2,1)}, bf16[256,1280]{1,0:T(8,128)(2,1)}, u32[]{:S(2)}, u32[]{:S(2)}) collective-permute-start(bf16[256,1280]{1,0:T(8,128)(2,1)} %get-tuple-element.625), channel_id=1, source_target_pairs={{0,24},{1,25},{2,26},{3,27},{4,28},{5,29},{6,30},{7,31}} | collective-permute-start | bytes 1966088 | tf_op jit(solution)/shard_map/while/body/eval_jaxpr/ppermute | solution.py:17
  196.9 10.1 %collective-permute-start = (bf16[256,1280]{1,0:T(8,128)(2,1)}, bf16[256,1280]{1,0:T(8,128)(2,1)S(1)}, u32[]{:S(2)}, u32[]{:S(2)}) collective-permute-start(bf16[256,1280]{1,0:T(8,128)(2,1)} %get-tuple-element.625), channel_id=1, source_target_pairs={{0,8},{8,16},{16,24},{1,9},{9,17},{17,25},{2,10},{10,18},{18,26},{... | collective-permute-start | bytes 1966088 | tf_op jit(solution)/shard_map/while/body/eval_jaxpr/ppermute | solution.py:17
  246.9 1.2 copy-start.1
Sparse Core Ops, SparseCore 0:
  248.2 98.4 reduce-scatter.1
where the time goes:
time: 356 us; the launch traced here: 355 us
  other arithmetic  97.1 us (27%)
  blocking collectives  76 us (21%)
  matrix products  54.3 us (15%)
  waiting for transfers between devices  48.4 us (14%)
  local copies, waits for them, and re-layouts  32.9 us (9%)
  starting transfers between devices  32.5 us (9%)
  between operations  13.5 us (4%)
    dot_general x5, matrix products, rms_block(): jnp.dot(hidden, w_second, preferred_element_type=jnp.float32)  46.7 us
    unnamed x1, blocking collectives  39.8 us
    scatter-add x1, other arithmetic, per_device(): sums = sums.at[band_high, slab_high, band_low, slab_low].add(placed)  38.8 us
    all_gather x1, blocking collectives, per_device(): panorama = lax.all_gather(latent, 'win', axis=1, tiled=True)  36.2 us
    scatter-add x1, other arithmetic, per_device(): counts = counts.at[band_high, slab_high, band_low, slab_low].add(live)  35.2 us
    ppermute x10, starting transfers between devices, shifted(): lax.ppermute(value, axis, [(source, source + steps) for source in range(l...  32.5 us
    ppermute x10, waiting for transfers between devices, shifted(): lax.ppermute(value, axis, [(source, source + steps) for source in range(l...  24.8 us
    reduce_scatter x1, waiting for transfers between devices, per_device(): lax.psum_scatter(sums.reshape(sections * slabs, band, slab_width, feat_di...  23.5 us
  transfers between devices with their start and end apart: 11, of which 6 were waited for; matrix products, arithmetic and copies ran while one was open for 16% of the time, Pallas kernels for 0%

commit v1 on v0

v1 whole, which is shorter than its diff:
```python
import functools

import jax
import jax.numpy as jnp
from jax import lax
from jax.experimental import pallas as pl
from jax.experimental.pallas import tpu as pltpu
from jax.sharding import PartitionSpec as P

MESH = pl.DeviceIdType.MESH
TILE = 16
MB = 128
PIECES = 5


def gelu(x):
    return 0.5 * x * (1.0 + jnp.tanh(0.7978845608028654 * (x + 0.044715 * (x * x * x))))


def kernel(
    sections, slabs, height, width,
    latent, anchors, in_proj, pos_embed, w1_in, w2_in, gain_in, skip_in, out_in,
    result,
    panel, cast, marks, w1, w2, skip, proj, pos, outp, gain,
    received, skipped, produced, value, normed, sums, blocks, arrived,
    load_sem, mark_send, mark_recv, slab_send, slab_recv,
    next_send, next_recv, skip_send, skip_recv, done_send, done_recv,
):
    section = lax.axis_index("section")
    win = lax.axis_index("win")
    last = sections - 1
    count, rows = received.shape[0], received.shape[1]
    tokens = TILE * TILE
    half = height * width
    band = half // sections
    hidden = w1.shape[1]
    model = w1.shape[0]
    piece = hidden // PIECES
    after = lax.rem(win + 1, slabs)
    before = lax.rem(win + slabs - 1, slabs)

    def load(source, target, index):
        return pltpu.make_async_copy(source, target, load_sem.at[index])

    def w1_load(p):
        return load(w1_in.at[0, pl.ds(p * (model // PIECES), model // PIECES)],
                    w1.at[pl.ds(p * (model // PIECES), model // PIECES)], p)

    def w2_load(p):
        return load(w2_in.at[0, pl.ds(p * piece, piece)], w2.at[pl.ds(p * piece, piece)], PIECES + p)

    base = 2 * PIECES
    gain_load = load(gain_in, gain, base)
    proj_load = load(in_proj, proj, base + 1)
    pos_load = load(pos_embed, pos, base + 2)
    skip_load = load(skip_in, skip, base + 3)
    out_load = load(out_in, outp, base + 4)
    own_load = load(latent, panel.at[0], base + 5)

    barrier = pltpu.get_barrier_semaphore()

    def greet(to_section, to_win):
        pl.semaphore_signal(barrier, inc=1, device_id=(to_section, to_win), device_id_type=MESH)

    def greet_peer(step, carry):
        greet(section, lax.rem(win + step, slabs))
        return carry

    lax.fori_loop(1, slabs, greet_peer, 0)

    @pl.when(section > 0)
    def _():
        greet(section - 1, win)

    @pl.when(section == last)
    def _():
        greet(0, win)

    @pl.when(section < last)
    def _():
        greet(last, win)
        greet(last, before)

    @pl.when(section == 0)
    def _():
        own_load.start()
        proj_load.start()
        pos_load.start()

    gain_load.start()
    for p in range(PIECES):
        w1_load(p).start()
    for p in range(PIECES):
        w2_load(p).start()

    @pl.when(section == last)
    def _():
        skip_load.start()
        out_load.start()

    line = lax.broadcasted_iota(jnp.int32, (16, 128), 0)
    block = jnp.full((16, 128), -4096, jnp.int32)
    for i in range(anchors.shape[0]):
        block = jnp.where(line == i, anchors[i, 0], block)
        block = jnp.where(line == 8 + i, anchors[i, 1], block)
    marks[win] = block.astype(jnp.float32)

    @pl.when(section == 0)
    def _():
        pl.semaphore_wait(barrier, slabs - 1 + 2)

    @pl.when((section > 0) & (section < last))
    def _():
        pl.semaphore_wait(barrier, slabs - 1 + 1)

    @pl.when(section == last)
    def _():
        pl.semaphore_wait(barrier, slabs - 1 + 2 * last)

    def slab_copy():
        return pltpu.make_async_remote_copy(
            src_ref=latent, dst_ref=panel.at[1], send_sem=slab_send, recv_sem=slab_recv,
            device_id=(section, before), device_id_type=MESH)

    @pl.when(section == 0)
    def _():
        slab_copy().start()

    def mark_copy(step):
        return pltpu.make_async_remote_copy(
            src_ref=marks.at[win], dst_ref=marks.at[win],
            send_sem=mark_send.at[step], recv_sem=mark_recv.at[step],
            device_id=(section, lax.rem(win + step, slabs)), device_id_type=MESH)

    def mark_start(step, carry):
        mark_copy(step).start()
        return carry

    def mark_wait(step, carry):
        origin = lax.rem(win - step + slabs, slabs)
        pltpu.make_async_remote_copy(
            src_ref=marks.at[origin], dst_ref=marks.at[origin],
            send_sem=mark_send.at[step], recv_sem=mark_recv.at[step],
            device_id=(section, lax.rem(win + step, slabs)), device_id_type=MESH).wait_recv()
        return carry

    lax.fori_loop(1, slabs, mark_start, 0)
    lax.fori_loop(1, slabs, mark_wait, 0)

    def row_anchors(group):
        every = marks[...]
        row, col = every[:, 0:8, :], every[:, 8:16, :]
        match = col == (group * width).astype(jnp.float32)
        low = jnp.min(jnp.min(jnp.where(match, row, 4096.0), axis=0), axis=0, keepdims=True)
        high = jnp.max(jnp.max(jnp.where(match, row, -4096.0), axis=0), axis=0, keepdims=True)
        return low[:, 0:1], high[:, 0:1]

    low, high = row_anchors(win)

    def place(index, shape, dim):
        anchor = jnp.where(index < count // 2, low, high)
        inside = lax.rem(index, count // 2) * rows
        token = lax.broadcasted_iota(jnp.int32, shape, dim) + inside
        row, col = token // TILE, token % TILE
        fixed = (row * width + col % width + half * (col // width)).astype(jnp.float32)
        spot = lax.broadcasted_iota(jnp.int32, shape, 1 - dim).astype(jnp.float32)
        return (spot == fixed + anchor * float(width)).astype(jnp.bfloat16)

    def dot(a, b):
        return jnp.dot(a, b, preferred_element_type=jnp.float32)

    def rms_block():
        v = value[...]
        factor = lax.rsqrt(jnp.mean(v * v, axis=-1, keepdims=True) + 1e-06)
        normed[...] = (v * factor * gain[...]).astype(jnp.bfloat16)
        for p in range(PIECES):
            part = gelu(dot(normed[...], w1[:, p * piece:(p + 1) * piece])).astype(jnp.bfloat16)
            value[...] += dot(part, w2[p * piece:(p + 1) * piece, :])
        return value[...].astype(jnp.bfloat16)

    def next_copy(index, target):
        return pltpu.make_async_remote_copy(
            src_ref=produced.at[index], dst_ref=received.at[index],
            send_sem=next_send.at[index], recv_sem=next_recv.at[index],
            device_id=(target, win), device_id_type=MESH)

    def skip_copy(index):
        return pltpu.make_async_remote_copy(
            src_ref=produced.at[index], dst_ref=skipped.at[index],
            send_sem=skip_send.at[index], recv_sem=skip_recv.at[index],
            device_id=(last, win), device_id_type=MESH)

    def wait_weights():
        gain_load.wait()
        for p in range(PIECES):
            w1_load(p).wait()
        for p in range(PIECES):
            w2_load(p).wait()

    @pl.when(section == 0)
    def _():
        own_load.wait()
        proj_load.wait()
        pos_load.wait()
        slab_copy().wait_recv()
        both = jnp.concatenate([panel[0], panel[1]], axis=0)
        cast[...] = both
        wait_weights()

        def step(index, carry):
            tiles = dot(place(index, (rows, 2 * half), 0), cast[...]).astype(jnp.bfloat16)
            start = pl.multiple_of(lax.rem(index, count // 2) * rows, rows)
            value[...] = dot(tiles, proj[...]) + pos[pl.ds(start, rows), :].astype(jnp.float32)
            produced[index] = rms_block()
            next_copy(index, 1).start()
            skip_copy(index).start()
            return carry

        lax.fori_loop(0, count, step, 0)

        def drain(index, carry):
            next_copy(index, 1).wait_send()
            skip_copy(index).wait_send()
            return carry

        lax.fori_loop(0, count, drain, 0)
        slab_copy().wait_send()

    @pl.when((section > 0) & (section < last))
    def _():
        wait_weights()

        def step(index, carry):
            next_copy(index, section + 1).wait_recv()
            value[...] = received[index].astype(jnp.float32)
            produced[index] = rms_block()
            next_copy(index, section + 1).start()
            return carry

        lax.fori_loop(0, count, step, 0)

        def drain(index, carry):
            next_copy(index, section + 1).wait_send()
            return carry

        lax.fori_loop(0, count, drain, 0)

    def done_copy(target, side):
        return pltpu.make_async_remote_copy(
            src_ref=blocks.at[pl.ds(pl.multiple_of((side * sections + target) * band, 16), band)],
            dst_ref=arrived.at[side],
            send_sem=done_send.at[side, target], recv_sem=done_recv.at[side],
            device_id=(target, after if side else win), device_id_type=MESH)

    @pl.when(section == last)
    def _():
        wait_weights()
        skip_load.wait()
        out_load.wait()
        sums[...] = jnp.zeros_like(sums)

        def step(index, carry):
            next_copy(index, 0).wait_recv()
            skip_copy(index).wait_recv()
            value[...] = dot(received[index], skip[:model, :]) + dot(skipped[index], skip[model:, :])
            noise = dot(rms_block(), outp[...]).astype(jnp.bfloat16)
            sums[...] += dot(place(index, (2 * half, rows), 1), noise)
            return carry

        lax.fori_loop(0, count, step, 0)
        blocks[...] = sums[...].astype(jnp.bfloat16)
        for target in range(sections):
            done_copy(target, 1).start()
        for target in range(sections - 1):
            done_copy(target, 0).start()
        arrived[0] = blocks[pl.ds(last * band, band), :]

    lowest, highest = row_anchors(before)
    line = lax.broadcasted_iota(jnp.int32, (band, 128), 0) // width + section * (height // sections)
    line = line.astype(jnp.float32)
    covered = jnp.zeros((band, 128), jnp.float32)
    for anchor in (low, high, lowest, highest):
        covered += jnp.where((line >= anchor) & (line < anchor + float(TILE)), 1.0, 0.0)

    @pl.when(section < last)
    def _():
        done_copy(0, 0).wait_recv()

    done_copy(0, 1).wait_recv()
    total = arrived[0].astype(jnp.float32) + arrived[1].astype(jnp.float32)
    result[...] = (total / covered[:, 0:1]).astype(jnp.bfloat16)

    @pl.when(section == last)
    def _():
        for target in range(sections):
            done_copy(target, 1).wait_send()
        for target in range(sections - 1):
            done_copy(target, 0).wait_send()

    def mark_drain(step, carry):
        mark_copy(step).wait_send()
        return carry

    lax.fori_loop(1, slabs, mark_drain, 0)


def solution(mesh):
    sections, slabs = mesh.shape["section"], mesh.shape["win"]

    def per_device(latent, anchors, in_proj, pos_embed, w1, w2, gain, skip_w, out_proj):
        height, width, feat = latent.shape
        model, hidden = w1.shape[1:]
        half = height * width
        band = half // sections
        rows = MB
        count = anchors.shape[0] * TILE * TILE // rows
        bf16, f32 = jnp.bfloat16, jnp.float32
        hbm = pl.BlockSpec(memory_space=pl.ANY)
        dma = pltpu.SemaphoreType.DMA
        out = pl.pallas_call(
            functools.partial(kernel, sections, slabs, height, width),
            out_shape=jax.ShapeDtypeStruct((band, feat), bf16),
            in_specs=[hbm, pl.BlockSpec(memory_space=pltpu.SMEM)] + [hbm] * 7,
            out_specs=pl.BlockSpec(memory_space=pltpu.VMEM),
            scratch_shapes=[
                pltpu.VMEM((2, half, feat), bf16),
                pltpu.VMEM((2 * half, feat), bf16),
                pltpu.VMEM((slabs, 16, 128), f32),
                pltpu.VMEM((model, hidden), bf16),
                pltpu.VMEM((hidden, model), bf16),
                pltpu.VMEM((2 * model, model), bf16),
                pltpu.VMEM((feat, model), bf16),
                pltpu.VMEM((TILE * TILE, model), bf16),
                pltpu.VMEM((model, feat), bf16),
                pltpu.VMEM((1, model), f32),
                pltpu.VMEM((count, rows, model), bf16),
                pltpu.VMEM((count, rows, model), bf16),
                pltpu.VMEM((count, rows, model), bf16),
                pltpu.VMEM((rows, model), f32),
                pltpu.VMEM((rows, model), bf16),
                pltpu.VMEM((2 * half, feat), f32),
                pltpu.VMEM((2 * half, feat), bf16),
                pltpu.VMEM((2, band, feat), bf16),
                dma((2 * PIECES + 6,)),
                dma((slabs,)),
                dma((slabs,)),
                dma,
                dma,
                dma((count,)),
                dma((count,)),
                dma((count,)),
                dma((count,)),
                dma((2, sections)),
                dma((2,)),
            ],
            compiler_params=pltpu.CompilerParams(
                collective_id=0, has_side_effects=True, vmem_limit_bytes=56 * 1024 * 1024),
        )(latent.reshape(half, feat), anchors, in_proj, pos_embed, w1, w2, gain, skip_w, out_proj)
        return out.reshape(height // sections, width, feat)

    return jax.shard_map(
        per_device,
        mesh=mesh,
        in_specs=(
            P(None, "win", None), P("win", None), P(), P(), P("section", None, None),
            P("section", None, None), P("section", None), P(), P(),
        ),
        out_specs=P("section", "win", None),
        check_vma=False,
    )
```

time: 356 us -> 63.1 us (0.18)
  other arithmetic: 97.1 us -> 0 us
  blocking collectives: 76 us -> 0 us
  Pallas kernels: 0 us -> 61.6 us
  matrix products: 54.3 us -> 0 us
  waiting for transfers between devices: 48.4 us -> 0 us
  starting transfers between devices: 32.5 us -> 0 us
  local copies, waits for them, and re-layouts: 32.9 us -> 1.35 us
  between operations: 13.5 us -> 0.01 us
    scatter-add x2 -> x0, other arithmetic: 74 us -> none  [the longest x1 38.8 us: per_device(): sums = sums.at[band_high, slab_high, band_low, slab_low].add(placed)]
    pallas_call x0 -> x1, Pallas kernels: none -> 61.6 us  [per_device(): pl.pallas_call(functools.partial(kernel, sections, slabs, height, width),...]
    dot_general x10 -> x0, matrix products: 54.3 us -> none  [the longest x5 46.7 us: rms_block(): jnp.dot(hidden, w_second, preferred_element_type=jnp.float32)]
    unnamed x1 -> x0, blocking collectives: 39.8 us -> none
    all_gather x1 -> x0, blocking collectives: 36.2 us -> none  [per_device(): panorama = lax.all_gather(latent, 'win', axis=1, tiled=True)]
    ppermute x10 -> x0, starting transfers between devices: 32.5 us -> none  [shifted(): lax.ppermute(value, axis, [(source, source + steps) for source in range(l...]
    ppermute x10 -> x0, waiting for transfers between devices: 24.8 us -> none  [shifted(): lax.ppermute(value, axis, [(source, source + steps) for source in range(l...]
    reduce_scatter x1 -> x0, waiting for transfers between devices: 23.5 us -> none  [per_device(): lax.psum_scatter(sums.reshape(sections * slabs, band, slab_width, feat_di...]
  transfers between devices with their start and end apart: 11 -> 0, of which waited for: 6 -> 0; matrix products, arithmetic and copies ran while one was open for 16% -> 0% of each run, Pallas kernels for 0% -> 0%
where the time goes in v1:
time: 63.1 us; the launch traced here: 62.9 us
  Pallas kernels  61.6 us (98%)
  local copies, waits for them, and re-layouts  1.35 us (2%)
    pallas_call x1, Pallas kernels, per_device(): pl.pallas_call(functools.partial(kernel, sections, slabs, height, width),...  61.6 us
    unnamed x1, local copies, waits for them, and re-layouts  1.35 us

profile of v1, /device:TPU:0, one launch (start us, length us, event | category | flops | bytes accessed | tf_op | source)
XLA Modules:
  0.0 62.9 jit_solution(8072226918309660788)
XLA Ops:
  0.0 61.6 %shard_map.91 = bf16[48,256]{1,0:T(8,128)(2,1)} custom-call(bf16[192,256]{1,0:T(8,128)(2,1)} %bitcast.2, s32[2,2]{1,0:T(2,128)} %anchors.1, bf16[256,1280]{1,0:T(8,128)(2,1)} %in_proj.1, bf16[256,1280]{1,0:T(8,128)(2,1)} %pos_embed.1, bf16[1,1280,2560]{2,1,0:T(8,128)(2,1)} %w1_in.1, bf16[1,2560,1280]{2,1,0:T(8,128)(2,1)} %w2_in.1, f32[1,1280]{1,0:T(1,128)} %gain_in.1, ...), custom_call_target="tpu_custom_call" | custom-call | tf_op jit(solution)/shard_map/pallas_call | solution.py:320
  61.6 1.3 %copy.11 = bf16[6,8,256]{2,1,0:T(8,128)(2,1)} copy(bf16[6,8,256]{2,1,0:T(8,128)(2,1)} %bitcast.3) | data formatting | bytes 49152

commit v2 on v1

--- a/solution.py
+++ b/solution.py
@@ -24,7 +24,7 @@
     panel, cast, marks, w1, w2, skip, proj, pos, outp, gain,
     received, skipped, produced, value, normed, sums, blocks, arrived,
     load_sem, mark_send, mark_recv, slab_send, slab_recv,
-    next_send, next_recv, skip_send, skip_recv, done_send, done_recv,
+    next_send, next_recv, skip_send, skip_recv, done_send, done_recv, credit,
 ):
     section = lax.axis_index("section")
     win = lax.axis_index("win")
@@ -76,6 +76,10 @@
     def _():
         greet(0, win)
 
+    @pl.when(section == 0)
+    def _():
+        greet(1, win)
+
     @pl.when(section < last)
     def _():
         greet(last, win)
@@ -109,7 +113,11 @@
     def _():
         pl.semaphore_wait(barrier, slabs - 1 + 2)
 
-    @pl.when((section > 0) & (section < last))
+    @pl.when(section == 1)
+    def _():
+        pl.semaphore_wait(barrier, slabs - 1 + 2)
+
+    @pl.when((section > 1) & (section < last))
     def _():
         pl.semaphore_wait(barrier, slabs - 1 + 1)
 
@@ -213,10 +221,17 @@
             value[...] = dot(tiles, proj[...]) + pos[pl.ds(start, rows), :].astype(jnp.float32)
             produced[index] = rms_block()
             next_copy(index, 1).start()
+
+            @pl.when(index == 0)
+            def _():
+                skip_copy(index).start()
+
+            return carry
+
+        lax.fori_loop(0, count, step, 0)
+        for index in range(1, count):
+            pl.semaphore_wait(credit, 1 if index < count - 1 else 2)
             skip_copy(index).start()
-            return carry
-
-        lax.fori_loop(0, count, step, 0)
 
         def drain(index, carry):
             next_copy(index, 1).wait_send()
@@ -235,15 +250,22 @@
             value[...] = received[index].astype(jnp.float32)
             produced[index] = rms_block()
             next_copy(index, section + 1).start()
+
+            @pl.when(index > 0)
+            def _():
+                left(index - 1)
+
             return carry
 
+        def left(index):
+            next_copy(index, section + 1).wait_send()
+
+            @pl.when(section == 1)
+            def _():
+                pl.semaphore_signal(credit, inc=1, device_id=(0, win), device_id_type=MESH)
+
         lax.fori_loop(0, count, step, 0)
-
-        def drain(index, carry):
-            next_copy(index, section + 1).wait_send()
-            return carry
-
-        lax.fori_loop(0, count, drain, 0)
+        left(count - 1)
 
     def done_copy(target, side):
         return pltpu.make_async_remote_copy(
@@ -261,8 +283,9 @@
 
         def step(index, carry):
             next_copy(index, 0).wait_recv()
+            value[...] = dot(received[index], skip[:model, :])
             skip_copy(index).wait_recv()
-            value[...] = dot(received[index], skip[:model, :]) + dot(skipped[index], skip[model:, :])
+            value[...] += dot(skipped[index], skip[model:, :])
             noise = dot(rms_block(), outp[...]).astype(jnp.bfloat16)
             sums[...] += dot(place(index, (2 * half, rows), 1), noise)
             return carry
@@ -352,6 +375,7 @@
                 dma((count,)),
                 dma((2, sections)),
                 dma((2,)),
+                pltpu.SemaphoreType.REGULAR,
             ],
             compiler_params=pltpu.CompilerParams(
                 collective_id=0, has_side_effects=True, vmem_limit_bytes=56 * 1024 * 1024),

time: 63.1 us -> 58.8 us (0.932)
  Pallas kernels: 61.6 us -> 57.3 us
    pallas_call x1, Pallas kernels: 61.6 us -> 57.3 us  [per_device(): pl.pallas_call(functools.partial(kernel, sections, slabs, height, width),...]
where the time goes in v2:
time: 58.8 us; the launch traced here: 58.6 us
  Pallas kernels  57.3 us (97%)
  local copies, waits for them, and re-layouts  1.35 us (2%)
    pallas_call x1, Pallas kernels, per_device(): pl.pallas_call(functools.partial(kernel, sections, slabs, height, width),...  57.3 us
    unnamed x1, local copies, waits for them, and re-layouts  1.35 us

profile of v2, /device:TPU:0, one launch (start us, length us, event | category | flops | bytes accessed | tf_op | source)
XLA Modules:
  0.0 58.6 jit_solution(11330038338550066011)
XLA Ops:
  0.0 57.3 %shard_map.91 = bf16[48,256]{1,0:T(8,128)(2,1)} custom-call(bf16[192,256]{1,0:T(8,128)(2,1)} %bitcast.2, s32[2,2]{1,0:T(2,128)} %anchors.1, bf16[256,1280]{1,0:T(8,128)(2,1)} %in_proj.1, bf16[256,1280]{1,0:T(8,128)(2,1)} %pos_embed.1, bf16[1,1280,2560]{2,1,0:T(8,128)(2,1)} %w1_in.1, bf16[1,2560,1280]{2,1,0:T(8,128)(2,1)} %w2_in.1, f32[1,1280]{1,0:T(1,128)} %gain_in.1, ...), custom_call_target="tpu_custom_call" | custom-call | tf_op jit(solution)/shard_map/pallas_call | solution.py:343
  57.3 1.3 %copy.11 = bf16[6,8,256]{2,1,0:T(8,128)(2,1)} copy(bf16[6,8,256]{2,1,0:T(8,128)(2,1)} %bitcast.3) | data formatting | bytes 49152

commit v3 on v2

--- a/solution.py
+++ b/solution.py
@@ -11,6 +11,7 @@
 TILE = 16
 MB = 128
 PIECES = 5
+PARTS = 5
 
 
 def gelu(x):
@@ -22,14 +23,15 @@
     latent, anchors, in_proj, pos_embed, w1_in, w2_in, gain_in, skip_in, out_in,
     result,
     panel, cast, marks, w1, w2, skip, proj, pos, outp, gain,
-    received, skipped, produced, value, normed, sums, blocks, arrived,
+    received, skipped, produced, value, normed, units, sums, blocks, arrived,
     load_sem, mark_send, mark_recv, slab_send, slab_recv,
     next_send, next_recv, skip_send, skip_recv, done_send, done_recv, credit,
 ):
     section = lax.axis_index("section")
     win = lax.axis_index("win")
     last = sections - 1
-    count, rows = received.shape[0], received.shape[1]
+    count, rows = received.shape[0], received.shape[2]
+    wide = received.shape[3]
     tokens = TILE * TILE
     half = height * width
     band = half // sections
@@ -177,33 +179,49 @@
     def dot(a, b):
         return jnp.dot(a, b, preferred_element_type=jnp.float32)
 
-    def rms_block():
+    def joined(ref, index):
+        return jnp.concatenate([ref[index, p] for p in range(PARTS)], axis=1)
+
+    def rms_block(emit, between=None):
         v = value[...]
         factor = lax.rsqrt(jnp.mean(v * v, axis=-1, keepdims=True) + 1e-06)
         normed[...] = (v * factor * gain[...]).astype(jnp.bfloat16)
         for p in range(PIECES):
-            part = gelu(dot(normed[...], w1[:, p * piece:(p + 1) * piece])).astype(jnp.bfloat16)
-            value[...] += dot(part, w2[p * piece:(p + 1) * piece, :])
-        return value[...].astype(jnp.bfloat16)
-
-    def next_copy(index, target):
+            part = gelu(dot(normed[...], w1[:, p * piece:(p + 1) * piece]))
+            units[:, p * piece:(p + 1) * piece] = part.astype(jnp.bfloat16)
+        if between is not None:
+            between()
+        for p in range(PARTS):
+            here = slice(p * wide, (p + 1) * wide)
+            emit(p, (value[:, here] + dot(units[...], w2[:, here])).astype(jnp.bfloat16))
+
+    def cut(ref, index, p):
+        return ref.at[index] if p is None else ref.at[index, p]
+
+    def next_copy(index, target, p=None):
         return pltpu.make_async_remote_copy(
-            src_ref=produced.at[index], dst_ref=received.at[index],
+            src_ref=cut(produced, index, p), dst_ref=cut(received, index, p),
             send_sem=next_send.at[index], recv_sem=next_recv.at[index],
             device_id=(target, win), device_id_type=MESH)
 
-    def skip_copy(index):
+    def skip_copy(index, p=None):
         return pltpu.make_async_remote_copy(
-            src_ref=produced.at[index], dst_ref=skipped.at[index],
+            src_ref=cut(produced, index, p), dst_ref=cut(skipped, index, p),
             send_sem=skip_send.at[index], recv_sem=skip_recv.at[index],
             device_id=(last, win), device_id_type=MESH)
 
-    def wait_weights():
+    def wait_first():
         gain_load.wait()
         for p in range(PIECES):
             w1_load(p).wait()
+
+    def wait_second():
         for p in range(PIECES):
             w2_load(p).wait()
+
+    def wait_weights():
+        wait_first()
+        wait_second()
 
     @pl.when(section == 0)
     def _():
@@ -213,25 +231,31 @@
         slab_copy().wait_recv()
         both = jnp.concatenate([panel[0], panel[1]], axis=0)
         cast[...] = both
-        wait_weights()
+        wait_first()
 
         def step(index, carry):
             tiles = dot(place(index, (rows, 2 * half), 0), cast[...]).astype(jnp.bfloat16)
             start = pl.multiple_of(lax.rem(index, count // 2) * rows, rows)
             value[...] = dot(tiles, proj[...]) + pos[pl.ds(start, rows), :].astype(jnp.float32)
-            produced[index] = rms_block()
-            next_copy(index, 1).start()
+
+            def emit(p, part):
+                produced[index, p] = part
+                next_copy(index, 1, p).start()
+
+            rms_block(emit, lambda: pl.when(index == 0)(wait_second))
 
             @pl.when(index == 0)
             def _():
-                skip_copy(index).start()
+                for p in range(PARTS):
+                    skip_copy(index, p).start()
 
             return carry
 
         lax.fori_loop(0, count, step, 0)
         for index in range(1, count):
             pl.semaphore_wait(credit, 1 if index < count - 1 else 2)
-            skip_copy(index).start()
+            for p in range(PARTS):
+                skip_copy(index, p).start()
 
         def drain(index, carry):
             next_copy(index, 1).wait_send()
@@ -247,9 +271,13 @@
 
         def step(index, carry):
             next_copy(index, section + 1).wait_recv()
-            value[...] = received[index].astype(jnp.float32)
-            produced[index] = rms_block()
-            next_copy(index, section + 1).start()
+            value[...] = joined(received, index).astype(jnp.float32)
+
+            def emit(p, part):
+                produced[index, p] = part
+                next_copy(index, section + 1, p).start()
+
+            rms_block(emit)
 
             @pl.when(index > 0)
             def _():
@@ -283,10 +311,15 @@
 
         def step(index, carry):
             next_copy(index, 0).wait_recv()
-            value[...] = dot(received[index], skip[:model, :])
+            value[...] = dot(joined(received, index), skip[:model, :])
             skip_copy(index).wait_recv()
-            value[...] += dot(skipped[index], skip[model:, :])
-            noise = dot(rms_block(), outp[...]).astype(jnp.bfloat16)
+            value[...] += dot(joined(skipped, index), skip[model:, :])
+
+            def emit(p, part):
+                normed[:, p * wide:(p + 1) * wide] = part
+
+            rms_block(emit)
+            noise = dot(normed[...], outp[...]).astype(jnp.bfloat16)
             sums[...] += dot(place(index, (2 * half, rows), 1), noise)
             return carry
 
@@ -356,11 +389,12 @@
                 pltpu.VMEM((TILE * TILE, model), bf16),
                 pltpu.VMEM((model, feat), bf16),
                 pltpu.VMEM((1, model), f32),
-                pltpu.VMEM((count, rows, model), bf16),
-                pltpu.VMEM((count, rows, model), bf16),
-                pltpu.VMEM((count, rows, model), bf16),
+                pltpu.VMEM((count, PARTS, rows, model // PARTS), bf16),
+                pltpu.VMEM((count, PARTS, rows, model // PARTS), bf16),
+                pltpu.VMEM((count, PARTS, rows, model // PARTS), bf16),
                 pltpu.VMEM((rows, model), f32),
                 pltpu.VMEM((rows, model), bf16),
+                pltpu.VMEM((rows, hidden), bf16),
                 pltpu.VMEM((2 * half, feat), f32),
                 pltpu.VMEM((2 * half, feat), bf16),
                 pltpu.VMEM((2, band, feat), bf16),

time: 58.8 us -> 57 us (0.969)
  Pallas kernels: 57.3 us -> 55.4 us
    pallas_call x1, Pallas kernels: 57.3 us -> 55.4 us  [per_device(): pl.pallas_call(functools.partial(kernel, sections, slabs, height, width),...]
where the time goes in v3:
time: 57 us; the launch traced here: 56.8 us
  Pallas kernels  55.4 us (97%)
  local copies, waits for them, and re-layouts  1.35 us (2%)
    pallas_call x1, Pallas kernels, per_device(): pl.pallas_call(functools.partial(kernel, sections, slabs, height, width),...  55.4 us
    unnamed x1, local copies, waits for them, and re-layouts  1.35 us

profile of v3, /device:TPU:0, one launch (start us, length us, event | category | flops | bytes accessed | tf_op | source)
XLA Modules:
  0.0 56.8 jit_solution(13940710990095580007)
XLA Ops:
  0.0 55.4 %shard_map.91 = bf16[48,256]{1,0:T(8,128)(2,1)} custom-call(bf16[192,256]{1,0:T(8,128)(2,1)} %bitcast.2, s32[2,2]{1,0:T(2,128)} %anchors.1, bf16[256,1280]{1,0:T(8,128)(2,1)} %in_proj.1, bf16[256,1280]{1,0:T(8,128)(2,1)} %pos_embed.1, bf16[1,1280,2560]{2,1,0:T(8,128)(2,1)} %w1_in.1, bf16[1,2560,1280]{2,1,0:T(8,128)(2,1)} %w2_in.1, f32[1,1280]{1,0:T(1,128)} %gain_in.1, ...), custom_call_target="tpu_custom_call" | custom-call | tf_op jit(solution)/shard_map/pallas_call | solution.py:376
  55.4 1.3 %copy.11 = bf16[6,8,256]{2,1,0:T(8,128)(2,1)} copy(bf16[6,8,256]{2,1,0:T(8,128)(2,1)} %bitcast.3) | data formatting | bytes 49152

commit v4 on v3

--- a/solution.py
+++ b/solution.py
@@ -55,7 +55,10 @@
     gain_load = load(gain_in, gain, base)
     proj_load = load(in_proj, proj, base + 1)
     pos_load = load(pos_embed, pos, base + 2)
-    skip_load = load(skip_in, skip, base + 3)
+
+    def skip_load(part):
+        return load(skip_in.at[pl.ds(part * model, model)], skip, base + 3)
+
     out_load = load(out_in, outp, base + 4)
     own_load = load(latent, panel.at[0], base + 5)
 
@@ -99,9 +102,16 @@
     for p in range(PIECES):
         w2_load(p).start()
 
+    @pl.when(section == 0)
+    def _():
+        skip_load(1).start()
+
+    @pl.when(section == last - 1)
+    def _():
+        skip_load(0).start()
+
     @pl.when(section == last)
     def _():
-        skip_load.start()
         out_load.start()
 
     line = lax.broadcasted_iota(jnp.int32, (16, 128), 0)
@@ -206,7 +216,7 @@
 
     def skip_copy(index, p=None):
         return pltpu.make_async_remote_copy(
-            src_ref=cut(produced, index, p), dst_ref=cut(skipped, index, p),
+            src_ref=cut(skipped, index, p), dst_ref=cut(skipped, index, p),
             send_sem=skip_send.at[index], recv_sem=skip_recv.at[index],
             device_id=(last, win), device_id_type=MESH)
 
@@ -246,6 +256,15 @@
 
             @pl.when(index == 0)
             def _():
+                skip_load(1).wait()
+
+            first = joined(produced, index)
+            for p in range(PARTS):
+                product = dot(first, skip[:, p * wide:(p + 1) * wide])
+                skipped[index, p] = product.astype(jnp.bfloat16)
+
+            @pl.when(index == 0)
+            def _():
                 for p in range(PARTS):
                     skip_copy(index, p).start()
 
@@ -265,19 +284,20 @@
         lax.fori_loop(0, count, drain, 0)
         slab_copy().wait_send()
 
-    @pl.when((section > 0) & (section < last))
-    def _():
+    def left(index):
+        next_copy(index, section + 1).wait_send()
+
+        @pl.when(section == 1)
+        def _():
+            pl.semaphore_signal(credit, inc=1, device_id=(0, win), device_id_type=MESH)
+
+    def middle(send):
         wait_weights()
 
         def step(index, carry):
             next_copy(index, section + 1).wait_recv()
             value[...] = joined(received, index).astype(jnp.float32)
-
-            def emit(p, part):
-                produced[index, p] = part
-                next_copy(index, section + 1, p).start()
-
-            rms_block(emit)
+            send(index)
 
             @pl.when(index > 0)
             def _():
@@ -285,15 +305,30 @@
 
             return carry
 
-        def left(index):
-            next_copy(index, section + 1).wait_send()
-
-            @pl.when(section == 1)
-            def _():
-                pl.semaphore_signal(credit, inc=1, device_id=(0, win), device_id_type=MESH)
-
         lax.fori_loop(0, count, step, 0)
         left(count - 1)
+
+    def send_part(index, p, part):
+        produced[index, p] = part
+        next_copy(index, section + 1, p).start()
+
+    @pl.when((section > 0) & (section < last - 1))
+    def _():
+        middle(lambda index: rms_block(functools.partial(send_part, index)))
+
+    @pl.when(section == last - 1)
+    def _():
+        def send(index):
+            def emit(p, part):
+                normed[:, p * wide:(p + 1) * wide] = part
+
+            rms_block(emit)
+            for p in range(PARTS):
+                product = dot(normed[...], skip[:, p * wide:(p + 1) * wide])
+                send_part(index, p, product.astype(jnp.bfloat16))
+
+        skip_load(0).wait()
+        middle(send)
 
     def done_copy(target, side):
         return pltpu.make_async_remote_copy(
@@ -305,15 +340,14 @@
     @pl.when(section == last)
     def _():
         wait_weights()
-        skip_load.wait()
         out_load.wait()
         sums[...] = jnp.zeros_like(sums)
 
         def step(index, carry):
             next_copy(index, 0).wait_recv()
-            value[...] = dot(joined(received, index), skip[:model, :])
             skip_copy(index).wait_recv()
-            value[...] += dot(joined(skipped, index), skip[model:, :])
+            value[...] = (joined(received, index).astype(jnp.float32)
+                          + joined(skipped, index).astype(jnp.float32))
 
             def emit(p, part):
                 normed[:, p * wide:(p + 1) * wide] = part
@@ -384,7 +418,7 @@
                 pltpu.VMEM((slabs, 16, 128), f32),
                 pltpu.VMEM((model, hidden), bf16),
                 pltpu.VMEM((hidden, model), bf16),
-                pltpu.VMEM((2 * model, model), bf16),
+                pltpu.VMEM((model, model), bf16),
                 pltpu.VMEM((feat, model), bf16),
                 pltpu.VMEM((TILE * TILE, model), bf16),
                 pltpu.VMEM((model, feat), bf16),

time: 57 us -> 57.3 us (level)
  no operation moved by 1% of the time
where the time goes in v4:
time: 57.3 us; the launch traced here: 57.1 us
  Pallas kernels  55.7 us (97%)
  local copies, waits for them, and re-layouts  1.35 us (2%)
    pallas_call x1, Pallas kernels, per_device(): pl.pallas_call(functools.partial(kernel, sections, slabs, height, width),...  55.7 us
    unnamed x1, local copies, waits for them, and re-layouts  1.35 us

profile of v4, /device:TPU:0, one launch (start us, length us, event | category | flops | bytes accessed | tf_op | source)
XLA Modules:
  0.0 57.1 jit_solution(11485416280108328588)
XLA Ops:
  0.0 55.7 %shard_map.91 = bf16[48,256]{1,0:T(8,128)(2,1)} custom-call(bf16[192,256]{1,0:T(8,128)(2,1)} %bitcast.2, s32[2,2]{1,0:T(2,128)} %anchors.1, bf16[256,1280]{1,0:T(8,128)(2,1)} %in_proj.1, bf16[256,1280]{1,0:T(8,128)(2,1)} %pos_embed.1, bf16[1,1280,2560]{2,1,0:T(8,128)(2,1)} %w1_in.1, bf16[1,2560,1280]{2,1,0:T(8,128)(2,1)} %w2_in.1, f32[1,1280]{1,0:T(1,128)} %gain_in.1, ...), custom_call_target="tpu_custom_call" | custom-call | tf_op jit(solution)/shard_map/pallas_call | solution.py:410
  55.7 1.3 %copy.11 = bf16[6,8,256]{2,1,0:T(8,128)(2,1)} copy(bf16[6,8,256]{2,1,0:T(8,128)(2,1)} %bitcast.3) | data formatting | bytes 49152

commit v5 on v4

--- a/solution.py
+++ b/solution.py
@@ -99,20 +99,6 @@
     gain_load.start()
     for p in range(PIECES):
         w1_load(p).start()
-    for p in range(PIECES):
-        w2_load(p).start()
-
-    @pl.when(section == 0)
-    def _():
-        skip_load(1).start()
-
-    @pl.when(section == last - 1)
-    def _():
-        skip_load(0).start()
-
-    @pl.when(section == last)
-    def _():
-        out_load.start()
 
     line = lax.broadcasted_iota(jnp.int32, (16, 128), 0)
     block = jnp.full((16, 128), -4096, jnp.int32)
@@ -165,6 +151,21 @@
         return carry
 
     lax.fori_loop(1, slabs, mark_start, 0)
+    for p in range(PIECES):
+        w2_load(p).start()
+
+    @pl.when((section == 0) | (section == last))
+    def _():
+        skip_load(1).start()
+
+    @pl.when(section == last - 1)
+    def _():
+        skip_load(0).start()
+
+    @pl.when(section == last)
+    def _():
+        out_load.start()
+
     lax.fori_loop(1, slabs, mark_wait, 0)
 
     def row_anchors(group):
@@ -252,29 +253,33 @@
                 produced[index, p] = part
                 next_copy(index, 1, p).start()
 
+                @pl.when(index == 0)
+                def _():
+                    skipped[0, p] = part
+                    skip_copy(0, p).start()
+
             rms_block(emit, lambda: pl.when(index == 0)(wait_second))
-
-            @pl.when(index == 0)
-            def _():
-                skip_load(1).wait()
-
+            return carry
+
+        lax.fori_loop(0, count, step, 0)
+        skip_load(1).wait()
+
+        def follow(index, carry):
             first = joined(produced, index)
             for p in range(PARTS):
                 product = dot(first, skip[:, p * wide:(p + 1) * wide])
                 skipped[index, p] = product.astype(jnp.bfloat16)
-
-            @pl.when(index == 0)
+            pl.semaphore_wait(credit, 1)
+
+            @pl.when(index == count - 1)
             def _():
-                for p in range(PARTS):
-                    skip_copy(index, p).start()
-
-            return carry
-
-        lax.fori_loop(0, count, step, 0)
-        for index in range(1, count):
-            pl.semaphore_wait(credit, 1 if index < count - 1 else 2)
+                pl.semaphore_wait(credit, 1)
+
             for p in range(PARTS):
                 skip_copy(index, p).start()
+            return carry
+
+        lax.fori_loop(1, count, follow, 0)
 
         def drain(index, carry):
             next_copy(index, 1).wait_send()
@@ -341,13 +346,22 @@
     def _():
         wait_weights()
         out_load.wait()
+        skip_load(1).wait()
         sums[...] = jnp.zeros_like(sums)
 
         def step(index, carry):
             next_copy(index, 0).wait_recv()
             skip_copy(index).wait_recv()
-            value[...] = (joined(received, index).astype(jnp.float32)
-                          + joined(skipped, index).astype(jnp.float32))
+            value[...] = joined(received, index).astype(jnp.float32)
+
+            @pl.when(index == 0)
+            def _():
+                value[...] += dot(joined(skipped, 0), skip[...])
+
+            @pl.when(index > 0)
+            def _():
+                value[...] += joined(skipped, index).astype(jnp.float32)
+
 
             def emit(p, part):
                 normed[:, p * wide:(p + 1) * wide] = part

time: 57.3 us -> 55.9 us (0.976)
  Pallas kernels: 55.7 us -> 54.3 us
    pallas_call x1, Pallas kernels: 55.7 us -> 54.3 us  [per_device(): pl.pallas_call(functools.partial(kernel, sections, slabs, height, width),...]
where the time goes in v5:
time: 55.9 us; the launch traced here: 55.7 us
  Pallas kernels  54.3 us (97%)
  local copies, waits for them, and re-layouts  1.35 us (2%)
    pallas_call x1, Pallas kernels, per_device(): pl.pallas_call(functools.partial(kernel, sections, slabs, height, width),...  54.3 us
    unnamed x1, local copies, waits for them, and re-layouts  1.35 us

profile of v5, /device:TPU:0, one launch (start us, length us, event | category | flops | bytes accessed | tf_op | source)
XLA Modules:
  0.0 55.7 jit_solution(13457780399631938871)
XLA Ops:
  0.0 54.3 %shard_map.91 = bf16[48,256]{1,0:T(8,128)(2,1)} custom-call(bf16[192,256]{1,0:T(8,128)(2,1)} %bitcast.2, s32[2,2]{1,0:T(2,128)} %anchors.1, bf16[256,1280]{1,0:T(8,128)(2,1)} %in_proj.1, bf16[256,1280]{1,0:T(8,128)(2,1)} %pos_embed.1, bf16[1,1280,2560]{2,1,0:T(8,128)(2,1)} %w1_in.1, bf16[1,2560,1280]{2,1,0:T(8,128)(2,1)} %w2_in.1, f32[1,1280]{1,0:T(1,128)} %gain_in.1, ...), custom_call_target="tpu_custom_call" | custom-call | tf_op jit(solution)/shard_map/pallas_call | solution.py:424
  54.4 1.3 %copy.11 = bf16[6,8,256]{2,1,0:T(8,128)(2,1)} copy(bf16[6,8,256]{2,1,0:T(8,128)(2,1)} %bitcast.3) | data formatting | bytes 49152
